TPU v7x, 128 devices: a whole 4x4x4 slice. The times are simulated.
128 devices in a mesh: outer: 8 (over y_hi, x), inner: 16 (over y_lo, z, core).
Axes of the slice: x: 4, y: 4 (y_hi: 2, y_lo: 2; y = y_hi * 2 + y_lo), z: 4, core: 2. Of those that a mesh axis runs over, the one named last changes fastest.
Arguments:
- pseudo_grad: float32 [8, 8192, 2048], P('outer', 'inner'), may hold values from -450 to 450, as said below
- params: float32 [8192, 2048], P('inner'), may hold values from -0.75 to 0.75
- momentum: float32 [8192, 2048], P('inner'), may hold values from -6 to 6
Outputs:
- new_params: float32 [8192, 2048], P('inner')
- new_momentum: float32 [8192, 2048], P('inner')
Inputs may be any that keep to these rules, and one draw needn't show every extreme that they name: `pseudo_grad`: finite real values.
All inputs are finite; a program needn't handle non-finite values.
Results may differ from a plain program's by a relative error of at most 0.00018.
Values sent between devices are 32-bit elements; how exact they have to be, the bound alone decides.
A program may use at most 64 MiB of HBM per device.

v0:
```python
import math

import jax
import jax.numpy as jnp
from jax import lax
from jax.sharding import PartitionSpec as P


def clip_factor(squares, entries):
    total_norm = jnp.sqrt(squares + 1e-06)
    return jnp.minimum(1.0, 0.5 * math.sqrt(entries) / total_norm)


def apply_update(clipped, params, momentum):
    new_momentum = 0.9 * momentum + clipped
    new_params = params - 0.7 * (clipped + 0.9 * new_momentum)
    return (new_params, new_momentum)


def per_device(pseudo_grad, params, momentum):
    groups = lax.axis_size("outer")
    entries = params.shape[0] * lax.axis_size("inner") * params.shape[1]
    local_grad = pseudo_grad[0]
    averaged = lax.psum(local_grad, "outer") / jnp.float32(groups)
    squares = lax.psum(jnp.sum(averaged * averaged), "inner")
    clipped = clip_factor(squares, entries) * averaged
    return apply_update(clipped, params, momentum)


def solution(mesh):
    placed = (P("outer", "inner", None), P("inner", None), P("inner", None))
    return jax.shard_map(
        per_device,
        mesh=mesh,
        in_specs=placed,
        out_specs=(P("inner", None), P("inner", None)),
        check_vma=False,
    )
```

profile of v0, /device:TPU:0, one launch (start us, length us, event | category | flops | bytes accessed | tf_op | source)
XLA Modules:
  0.0 174.8 jit_solution(17109028511441834021)
XLA Ops:
  7.2 0.0 all-reduce.2.cloned.1.call-start
  7.2 0.7 all-reduce.2.cloned.1.call-update
  7.9 114.9 %all-reduce.2.cloned.1.call-done = f32[512,2048]{1,0:T(8,128)} async-done(((f32[512,2048]{1,0:T(8,128)}), f32[512,2048]{1,0:T(8,128)}) %all-reduce.2.cloned.1.call-update) | async-done | bytes 4194320 | tf_op jit(solution)/shard_map/psum | solution.py:24
  122.8 3.9 %multiply_reduce_fusion = f32[]{:T(128)} fusion(f32[512,2048]{1,0:T(8,128)} %all-reduce.2.cloned.1.call-done), kind=kLoop, calls=%fused_computation.2 | loop fusion | flops 3145727 | bytes 4194308 | tf_op jit(solution)/shard_map/reduce_sum | solution.py:25
  126.7 30.2 %psum.15 = f32[]{:T(128)} all-reduce(f32[]{:T(128)} %multiply_reduce_fusion), channel_id=1, replica_groups=mesh['outer'=8,'inner'=16] {'inner'}, use_global_device_ids=true, to_apply=%region_2.0 | all-reduce | flops 1 | bytes 8 | tf_op jit(solution)/shard_map/psum | solution.py:25
  157.5 10.5 %multiply_subtract_fusion = (f32[512,2048]{1,0:T(8,128)}, f32[512,2048]{1,0:T(8,128)}) fusion(f32[512,2048]{1,0:T(8,128)} %param.4, f32[512,2048]{1,0:T(8,128)} %all-reduce.2.cloned.1.call-done, f32[]{:T(128)S(6)} %mul.24, f32[512,2048]{1,0:T(8,128)} %param.5), kind=kLoop, calls=%fused_computation | loop fusion | flops 7340032 | bytes 20971524 | tf_op jit(solution)/shard_map/sub | solution.py:16
Async XLA Ops:
  7.2 115.6 %all-reduce.2.cloned.1.call-start = ((), (), s32[]{:S(2)}) async-start(), calls=%async_computation | async-start | bytes 8388608 | tf_op jit(solution)/shard_map/psum | solution.py:24
Sparse Core Ops, SparseCore 0:
  10.5 112.2 all-reduce.1
where the time goes:
time: 175 us
  waiting for transfers between devices  116 us (66%)
  blocking collectives  30.2 us (17%)
  between operations  14.7 us (8%)
  other arithmetic  14.4 us (8%)
    psum x1, waiting for transfers between devices, per_device(): averaged = lax.psum(local_grad, 'outer') / jnp.float32(groups)  115 us
    psum x1, blocking collectives, per_device(): squares = lax.psum(jnp.sum(averaged * averaged), 'inner')  30.2 us
    sub x1, other arithmetic, apply_update(): new_params = params - 0.7 * (clipped + 0.9 * new_momentum)  10.5 us
    reduce_sum x1, other arithmetic, per_device(): squares = lax.psum(jnp.sum(averaged * averaged), 'inner')  3.87 us
  transfers between devices with their start and end apart: 1, of which 1 were waited for; matrix products, arithmetic and copies ran while one was open for 0% of the time, Pallas kernels for 0%

commit v1 on v0

v1 whole, which is shorter than its diff:
```python
import functools
import math

import jax
import jax.numpy as jnp
from jax import lax
from jax.experimental import pallas as pl
from jax.experimental.pallas import tpu as pltpu
from jax.sharding import PartitionSpec as P

MESH = pl.DeviceIdType.MESH
TILE = (8, 128)
TILES = 1024
A = 36
B = 28
STEP = 4
GROUPS = 8


def tiles_of(block):
    rows, columns = block.shape
    cut = block.reshape(rows // 8, 8, columns // 128, 128)
    return cut.transpose(0, 2, 1, 3).reshape(-1, 8, 128)


def block_of(tiles, rows, columns):
    cut = tiles.reshape(rows // 8, columns // 128, 8, 128)
    return cut.transpose(0, 2, 1, 3).reshape(rows, columns)


def over_tiles(count, body):
    def step(i, carry):
        body(pl.multiple_of(i * STEP, STEP))
        return carry

    lax.fori_loop(0, count // STEP, step, 0)


class Copies:
    def __init__(self, send_sem, recv_sem):
        self.send_sem, self.recv_sem, self.all = send_sem, recv_sem, []

    def send(self, src, dst, device):
        number = len(self.all)
        copy = pltpu.make_async_remote_copy(
            src_ref=src,
            dst_ref=dst,
            send_sem=self.send_sem.at[number],
            recv_sem=self.recv_sem.at[number],
            device_id=device,
            device_id_type=MESH,
        )
        copy.start()
        self.all.append(copy)
        return copy

    def finish(self):
        for copy in self.all:
            copy.wait_send()


COPIES = 65


def kernel(
    entries,
    grad_hbm,
    params_hbm,
    momentum_hbm,
    new_params,
    new_momentum,
    grad,
    params,
    momentum,
    mean,
    x_first,
    x_second,
    x_third,
    x_sum,
    x_from_y,
    y_sum,
    q_first,
    q_second,
    q_third,
    squares,
    norm_z,
    norm_core,
    norm_x,
    norm_y,
    send_sem,
    recv_sem,
    load_sem,
):
    outer, inner = lax.axis_index("outer"), lax.axis_index("inner")
    x, half = lax.rem(outer, 4), lax.div(outer, 4)
    low, z, core = lax.div(inner, 8), lax.rem(lax.div(inner, 2), 4), lax.rem(inner, 2)
    y = half * 2 + low

    def device(x=x, y=y, z=z, core=core):
        return (lax.div(y, 2) * 4 + x, (lax.rem(y, 2) * 4 + z) * 2 + core)

    def ring(at, by):
        return lax.rem(at + by, 4)

    east, west = device(x=ring(x, 1)), device(x=ring(x, 3))
    across = device(y=ring(y, 2))
    x_peers = [device(x=ring(x, k)) for k in (1, 2, 3)]
    y_peers = [device(y=ring(y, k)) for k in (1, 2, 3)]
    z_peers = [device(z=ring(z, k)) for k in (1, 2, 3)]
    core_peer = device(core=1 - core)

    barrier = pltpu.get_barrier_semaphore()
    peers = x_peers + y_peers + z_peers + [core_peer]
    for peer in peers:
        pl.semaphore_signal(barrier, inc=1, device_id=peer, device_id_type=MESH)
    loads = [
        pltpu.make_async_copy(src, dst, load_sem.at[i])
        for i, (src, dst) in enumerate(
            ((grad_hbm, grad), (params_hbm, params), (momentum_hbm, momentum))
        )
    ]
    loads[0].start()
    pl.semaphore_wait(barrier, len(peers))

    copies = Copies(send_sem, recv_sem)
    other = 1 - half

    def at_x(chunk, h, d, pieces=1):
        return pl.ds(((ring(x, chunk) * 2 + h) * 2 + d) * A, pieces * A)

    def at_y(h, chunk, d):
        return pl.ds(16 * A + ((h * 4 + ring(x, chunk)) * 2 + d) * B, B)

    def x_open(slot, h):
        return [
            copies.send(grad_hbm.at[at_x(2, h, 0)], x_first.at[slot, 0], west),
            copies.send(grad_hbm.at[at_x(2, h, 1)], x_first.at[slot, 1], east),
            copies.send(grad_hbm.at[at_x(1, h, 0)], x_second.at[slot, 0], east),
            copies.send(grad_hbm.at[at_x(3, h, 1)], x_second.at[slot, 1], west),
        ]

    def add_into(ref, term, start, count):
        def body(i):
            ref[pl.ds(i, STEP)] += term[pl.ds(start + i, STEP)]

        over_tiles(count, body)

    def x_pass(slot, h, opened):
        opened[1].wait_recv()
        add_into(x_first.at[slot, 1], grad, at_x(1, h, 1).start, A)
        one = copies.send(x_first.at[slot, 1], x_third.at[slot, 1], east)
        opened[0].wait_recv()
        add_into(x_first.at[slot, 0], grad, at_x(3, h, 0).start, A)
        two = copies.send(x_first.at[slot, 0], x_third.at[slot, 0], west)
        return [two, one]

    y_copies = {}

    def y_open(chunk, d):
        y_copies[chunk, d] = copies.send(
            grad_hbm.at[at_y(other, chunk, d)], y_sum.at[chunk * 2 + d], across
        )

    def y_add(chunk, d):
        y_copies[chunk, d].wait_recv()
        add_into(y_sum.at[chunk * 2 + d], grad, at_y(half, chunk, d).start, B)
        return y_sum.at[chunk * 2 + d]

    opened_a = x_open(0, other)
    y_open(2, 0)
    y_open(2, 1)
    y_open(1, 0)
    loads[1].start()
    loads[2].start()
    loads[0].wait()
    passed_a = x_pass(0, other, opened_a)
    y_open(3, 1)
    opened_b = x_open(1, half)
    y_open(1, 1)
    for d in (0, 1):
        opened_a[2 + d].wait_recv()
        passed_a[d].wait_recv()
        base = at_x(0, other, d).start

        def body(i, d=d, base=base):
            at = pl.ds(i, STEP)
            x_sum[d, at] = (
                grad[pl.ds(base + i, STEP)] + x_second[0, d, at] + x_third[0, d, at]
            )

        over_tiles(A, body)
        crossed = copies.send(x_sum.at[d], x_from_y.at[d], across)
        y_copies["x", d] = crossed
    y_open(3, 0)
    passed_b = x_pass(1, half, opened_b)
    y_open(0, 0)
    y_open(0, 1)
    q_opened = [
        copies.send(y_add(2, 0), q_first.at[0], west),
        copies.send(y_add(2, 1), q_first.at[1], east),
        copies.send(y_add(1, 0), q_second.at[0], east),
        copies.send(y_add(3, 1), q_second.at[1], west),
    ]
    y_add(1, 1)
    y_add(3, 0)

    squares[...] = jnp.zeros(TILE, jnp.float32)

    def store_mean(at, value):
        value = value / jnp.float32(GROUPS)
        mean[at] = value
        squares[...] += jnp.sum(value * value, axis=0)

    for d in (0, 1):
        opened_b[2 + d].wait_recv()
        passed_b[d].wait_recv()
        y_copies["x", d].wait_recv()
        base = at_x(0, half, d).start

        def body(i, d=d, base=base):
            at = pl.ds(i, STEP)
            own = grad[pl.ds(base + i, STEP)] + x_second[1, d, at] + x_third[1, d, at]
            store_mean(pl.ds(base + i, STEP), own + x_from_y[d, at])

        over_tiles(A, body)

    def gather(at, to):
        return copies.send(mean.at[at], mean.at[at], to)

    def x_gather(h):
        return [
            gather(at_x(0, h, 0), east),
            gather(at_x(0, h, 1), west),
            gather(at_x(0, h, 1), east),
            gather(at_x(0, h, 0), west),
        ]

    x_crossed = gather(at_x(0, half, 0, 2), across)
    x_own = x_gather(half)

    q_opened[1].wait_recv()
    add_into(q_first.at[1], y_sum.at[3], 0, B)
    q_east = copies.send(q_first.at[1], q_third.at[1], east)
    q_opened[0].wait_recv()
    add_into(q_first.at[0], y_sum.at[6], 0, B)
    q_west = copies.send(q_first.at[0], q_third.at[0], west)
    q_passed = [q_west, q_east]

    for d in (0, 1):
        y_add(0, d)
        q_opened[2 + d].wait_recv()
        q_passed[d].wait_recv()
        base = at_y(half, 0, d).start

        def body(i, d=d, base=base):
            at = pl.ds(i, STEP)
            store_mean(
                pl.ds(base + i, STEP), y_sum[d, at] + q_second[d, at] + q_third[d, at]
            )

        over_tiles(B, body)

    def norm_send(slots, mine, value, to):
        slots[mine] = value
        return [copies.send(slots.at[mine], slots.at[mine], peer) for peer in to]

    def norm_take(slots, sent):
        for copy in sent:
            copy.wait_recv()
        total = slots[0]
        for i in range(1, slots.shape[0]):
            total = total + slots[i]
        return total

    sent = norm_send(norm_z, z, squares[...], z_peers)
    q_own = [
        gather(at_y(half, 0, 0), east),
        gather(at_y(half, 0, 1), west),
        gather(at_y(half, 0, 1), east),
        gather(at_y(half, 0, 0), west),
    ]
    y_gathered = {}

    def y_gather(chunk, d):
        y_gathered[chunk, d] = gather(at_y(half, chunk, d), across)

    y_gather(0, 0)
    y_gather(0, 1)

    x_own[0].wait_recv()
    x_on = [gather(at_x(3, half, 0), east)]
    x_own[1].wait_recv()
    x_on += [gather(at_x(1, half, 1), west)]
    value = norm_take(norm_z, sent)
    sent = norm_send(norm_core, core, value, [core_peer])

    q_own[0].wait_recv()
    q_on = [gather(at_y(half, 3, 0), east)]
    y_gather(3, 0)
    q_own[1].wait_recv()
    q_on += [gather(at_y(half, 1, 1), west)]
    y_gather(1, 1)
    value = norm_take(norm_core, sent)
    sent = norm_send(norm_x, x, value, x_peers)
    q_own[2].wait_recv()
    y_gather(3, 1)
    q_own[3].wait_recv()
    y_gather(1, 0)
    x_crossed.wait_recv()
    x_far = x_gather(other)
    value = norm_take(norm_x, sent)
    sent = norm_send(norm_y, y, value, y_peers)
    q_on[0].wait_recv()
    y_gather(2, 0)
    q_on[1].wait_recv()
    y_gather(2, 1)
    x_far[0].wait_recv()
    x_far_on = [gather(at_x(3, other, 0), east)]
    x_far[1].wait_recv()
    x_far_on += [gather(at_x(1, other, 1), west)]
    total = norm_take(norm_y, sent)
    norm = jnp.sqrt(jnp.sum(total, keepdims=True) + 1e-06)
    factor = jnp.broadcast_to(
        jnp.minimum(1.0, 0.5 * math.sqrt(entries) / norm), TILE
    )[None]

    loads[1].wait()
    loads[2].wait()

    def update(at):
        start, count = at.start, at.size

        def body(i):
            at = pl.ds(start + i, STEP)
            clipped = factor * mean[at]
            moved = 0.9 * momentum[at] + clipped
            new_momentum[at] = moved
            new_params[at] = params[at] - 0.7 * (clipped + 0.9 * moved)

        over_tiles(count, body)

    update(at_x(0, half, 0, 2))
    update(at_x(3, half, 0))
    update(at_x(1, half, 1))
    x_own[2].wait_recv()
    update(at_x(3, half, 1))
    x_own[3].wait_recv()
    update(at_x(1, half, 0))
    x_on[0].wait_recv()
    update(at_x(2, half, 0))
    x_on[1].wait_recv()
    update(at_x(2, half, 1))
    update(at_x(0, other, 0, 2))
    for chunk in range(4):
        for d in (0, 1):
            update(at_y(half, chunk, d))
    order = ((0, 0), (0, 1), (3, 0), (1, 1), (3, 1), (1, 0))
    for chunk, d in order:
        y_gathered[chunk, d].wait_recv()
        update(at_y(other, chunk, d))
    update(at_x(3, other, 0))
    update(at_x(1, other, 1))
    x_far[2].wait_recv()
    update(at_x(3, other, 1))
    x_far[3].wait_recv()
    update(at_x(1, other, 0))
    for d in (0, 1):
        y_gathered[2, d].wait_recv()
        update(at_y(other, 2, d))
    x_far_on[0].wait_recv()
    update(at_x(2, other, 0))
    x_far_on[1].wait_recv()
    update(at_x(2, other, 1))
    copies.finish()


def store_kernel(params, momentum, params_out, momentum_out, sem):
    cuts = 4
    size = TILES // cuts
    copies = []
    for i in range(cuts):
        for j, (src, dst) in enumerate(((params, params_out), (momentum, momentum_out))):
            at = pl.ds(i * size, size)
            copy = pltpu.make_async_copy(src.at[at], dst.at[at], sem.at[i * 2 + j])
            copy.start()
            copies.append(copy)
    for copy in copies:
        copy.wait()


def per_device(pseudo_grad, params, momentum):
    rows, columns = params.shape
    entries = rows * lax.axis_size("inner") * columns
    f32 = jnp.float32
    near = pltpu.VMEM((TILES, *TILE), f32)
    far = jax.ShapeDtypeStruct((TILES, *TILE), f32)

    def vmem(*lead):
        return pltpu.VMEM((*lead, *TILE), f32)

    results = pl.pallas_call(
        functools.partial(kernel, entries),
        out_shape=[near, near],
        in_specs=[pl.BlockSpec(memory_space=pl.ANY)] * 3,
        out_specs=[pl.BlockSpec(memory_space=pltpu.VMEM)] * 2,
        scratch_shapes=[
            vmem(TILES),
            vmem(TILES),
            vmem(TILES),
            vmem(TILES),
            vmem(2, 2, A),
            vmem(2, 2, A),
            vmem(2, 2, A),
            vmem(2, A),
            vmem(2, A),
            vmem(8, B),
            vmem(2, B),
            vmem(2, B),
            vmem(2, B),
            vmem(),
            vmem(4),
            vmem(2),
            vmem(4),
            vmem(4),
            pltpu.SemaphoreType.DMA((COPIES,)),
            pltpu.SemaphoreType.DMA((COPIES,)),
            pltpu.SemaphoreType.DMA((3,)),
        ],
        compiler_params=pltpu.CompilerParams(
            collective_id=0, has_side_effects=True, vmem_limit_bytes=49 * 2**20
        ),
        name="outer_step",
    )(tiles_of(pseudo_grad[0]), tiles_of(params), tiles_of(momentum))
    results = pl.pallas_call(
        store_kernel,
        out_shape=[far, far],
        in_specs=[pl.BlockSpec(memory_space=pltpu.VMEM)] * 2,
        out_specs=[pl.BlockSpec(memory_space=pl.ANY)] * 2,
        scratch_shapes=[pltpu.SemaphoreType.DMA((8,))],
        compiler_params=pltpu.CompilerParams(vmem_limit_bytes=40 * 2**20),
        name="store",
    )(*results)
    return tuple(block_of(result, rows, columns) for result in results)


def solution(mesh):
    placed = (P("outer", "inner", None), P("inner", None), P("inner", None))
    return jax.shard_map(
        per_device,
        mesh=mesh,
        in_specs=placed,
        out_specs=(P("inner", None), P("inner", None)),
        check_vma=False,
    )
```

time: 175 us -> 69.3 us (0.40)
  waiting for transfers between devices: 116 us -> 0 us
  Pallas kernels: 0 us -> 68.6 us
  blocking collectives: 30.2 us -> 0 us
  other arithmetic: 14.4 us -> 0 us
  between operations: 14.7 us -> 0.64 us
    psum x1 -> x0, waiting for transfers between devices: 115 us -> none  [per_device(): averaged = lax.psum(local_grad, 'outer') / jnp.float32(groups)]
    pallas_call x0 -> x2, Pallas kernels: none -> 68.6 us  [the longest x1 65.2 us: per_device(): pl.pallas_call(functools.partial(kernel, entries), out_shape=[near, near]...]
    psum x1 -> x0, blocking collectives: 30.2 us -> none  [per_device(): squares = lax.psum(jnp.sum(averaged * averaged), 'inner')]
    sub x1 -> x0, other arithmetic: 10.5 us -> none  [apply_update(): new_params = params - 0.7 * (clipped + 0.9 * new_momentum)]
    reduce_sum x1 -> x0, other arithmetic: 3.87 us -> none  [per_device(): squares = lax.psum(jnp.sum(averaged * averaged), 'inner')]
  transfers between devices with their start and end apart: 1 -> 0, of which waited for: 1 -> 0; matrix products, arithmetic and copies ran while one was open for 0% -> 0% of each run, Pallas kernels for 0% -> 0%
where the time goes in v1:
time: 69.3 us; the launch traced here: 69.2 us
  Pallas kernels  68.6 us (99%)
    pallas_call x1, Pallas kernels, per_device(): pl.pallas_call(functools.partial(kernel, entries), out_shape=[near, near]...  65.2 us
    pallas_call x1, Pallas kernels, per_device(): pl.pallas_call(store_kernel, out_shape=[far, far], in_specs=[pl.BlockSpec...  3.37 us

profile of v1, /device:TPU:0, one launch (start us, length us, event | category | flops | bytes accessed | tf_op | source)
XLA Modules:
  0.0 69.2 jit_solution(7458209436161475112)
XLA Ops:
  0.6 65.2 %outer_step.1 = (f32[1024,8,128]{2,1,0:T(8,128)S(1)}, f32[1024,8,128]{2,1,0:T(8,128)S(1)}) custom-call(f32[1024,8,128]{2,1,0:T(8,128)} %bitcast.25, f32[1024,8,128]{2,1,0:T(8,128)} %bitcast.26, f32[1024,8,128]{2,1,0:T(8,128)} %bitcast.27), custom_call_target="tpu_custom_call" | custom-call | tf_op jit(solution)/shard_map/outer_step/pallas_call | solution.py:401
  65.9 3.4 %store.1 = (f32[1024,8,128]{2,1,0:T(8,128)}, f32[1024,8,128]{2,1,0:T(8,128)}) custom-call(f32[1024,8,128]{2,1,0:T(8,128)S(1)} %get-tuple-element.6.params, f32[1024,8,128]{2,1,0:T(8,128)S(1)} %get-tuple-element.7.momentum), custom_call_target="tpu_custom_call" | custom-call | tf_op jit(solution)/shard_map/store/pallas_call | solution.py:434

commit v2 on v1

--- a/solution.py
+++ b/solution.py
@@ -90,6 +90,7 @@
     send_sem,
     recv_sem,
     load_sem,
+    met_sem,
 ):
     outer, inner = lax.axis_index("outer"), lax.axis_index("inner")
     x, half = lax.rem(outer, 4), lax.div(outer, 4)
@@ -109,10 +110,21 @@
     z_peers = [device(z=ring(z, k)) for k in (1, 2, 3)]
     core_peer = device(core=1 - core)
 
+    met = [(ring(z, k) > z, device(z=ring(z, k))) for k in (1, 2, 3)]
+    met += [(ring(y, k) > y, device(y=ring(y, k))) for k in (1, 3)]
+    met += [(core == 0, core_peer)]
+    above = sum(jnp.where(later, 1, 0) for later, _ in met)
+
     barrier = pltpu.get_barrier_semaphore()
-    peers = x_peers + y_peers + z_peers + [core_peer]
-    for peer in peers:
+    group = [east, west, across]
+    for peer in group:
         pl.semaphore_signal(barrier, inc=1, device_id=peer, device_id_type=MESH)
+    for later, peer in met:
+
+        @pl.when(later)
+        def greet(peer=peer):
+            pl.semaphore_signal(barrier, inc=1, device_id=peer, device_id_type=MESH)
+
     loads = [
         pltpu.make_async_copy(src, dst, load_sem.at[i])
         for i, (src, dst) in enumerate(
@@ -120,7 +132,7 @@
         )
     ]
     loads[0].start()
-    pl.semaphore_wait(barrier, len(peers))
+    pl.semaphore_wait(barrier, len(group) + len(met) - above)
 
     copies = Copies(send_sem, recv_sem)
     other = 1 - half
@@ -170,6 +182,12 @@
     y_open(2, 0)
     y_open(2, 1)
     y_open(1, 0)
+    for later, peer in met:
+
+        @pl.when(jnp.logical_not(later))
+        def answer(peer=peer):
+            pl.semaphore_signal(met_sem, inc=1, device_id=peer, device_id_type=MESH)
+
     loads[1].start()
     loads[2].start()
     loads[0].wait()
@@ -271,6 +289,10 @@
         for i in range(1, slots.shape[0]):
             total = total + slots[i]
         return total
+
+    @pl.when(above > 0)
+    def all_met():
+        pl.semaphore_wait(met_sem, above)
 
     sent = norm_send(norm_z, z, squares[...], z_peers)
     q_own = [
@@ -425,6 +447,7 @@
             pltpu.SemaphoreType.DMA((COPIES,)),
             pltpu.SemaphoreType.DMA((COPIES,)),
             pltpu.SemaphoreType.DMA((3,)),
+            pltpu.SemaphoreType.REGULAR,
         ],
         compiler_params=pltpu.CompilerParams(
             collective_id=0, has_side_effects=True, vmem_limit_bytes=49 * 2**20

time: 69.3 us -> 67.4 us (0.973)
  Pallas kernels: 68.6 us -> 66.6 us
    pallas_call x1, Pallas kernels: 65.2 us -> 63.3 us  [per_device(): pl.pallas_call(functools.partial(kernel, entries), out_shape=[near, near]...]
where the time goes in v2:
time: 67.4 us; the launch traced here: 67.3 us
  Pallas kernels  66.6 us (99%)
    pallas_call x1, Pallas kernels, per_device(): pl.pallas_call(functools.partial(kernel, entries), out_shape=[near, near]...  63.3 us
    pallas_call x1, Pallas kernels, per_device(): pl.pallas_call(store_kernel, out_shape=[far, far], in_specs=[pl.BlockSpec...  3.37 us

profile of v2, /device:TPU:0, one launch (start us, length us, event | category | flops | bytes accessed | tf_op | source)
XLA Modules:
  0.0 67.3 jit_solution(164304804091246149)
XLA Ops:
  0.6 63.3 %outer_step.1 = (f32[1024,8,128]{2,1,0:T(8,128)S(1)}, f32[1024,8,128]{2,1,0:T(8,128)S(1)}) custom-call(f32[1024,8,128]{2,1,0:T(8,128)} %bitcast.25, f32[1024,8,128]{2,1,0:T(8,128)} %bitcast.26, f32[1024,8,128]{2,1,0:T(8,128)} %bitcast.27), custom_call_target="tpu_custom_call" | custom-call | tf_op jit(solution)/shard_map/outer_step/pallas_call | solution.py:423
  63.9 3.4 %store.1 = (f32[1024,8,128]{2,1,0:T(8,128)}, f32[1024,8,128]{2,1,0:T(8,128)}) custom-call(f32[1024,8,128]{2,1,0:T(8,128)S(1)} %get-tuple-element.6.params, f32[1024,8,128]{2,1,0:T(8,128)S(1)} %get-tuple-element.7.momentum), custom_call_target="tpu_custom_call" | custom-call | tf_op jit(solution)/shard_map/store/pallas_call | solution.py:457

commit v3 on v2

--- a/solution.py
+++ b/solution.py
@@ -157,15 +157,6 @@
 
         over_tiles(count, body)
 
-    def x_pass(slot, h, opened):
-        opened[1].wait_recv()
-        add_into(x_first.at[slot, 1], grad, at_x(1, h, 1).start, A)
-        one = copies.send(x_first.at[slot, 1], x_third.at[slot, 1], east)
-        opened[0].wait_recv()
-        add_into(x_first.at[slot, 0], grad, at_x(3, h, 0).start, A)
-        two = copies.send(x_first.at[slot, 0], x_third.at[slot, 0], west)
-        return [two, one]
-
     y_copies = {}
 
     def y_open(chunk, d):
@@ -178,10 +169,9 @@
         add_into(y_sum.at[chunk * 2 + d], grad, at_y(half, chunk, d).start, B)
         return y_sum.at[chunk * 2 + d]
 
-    opened_a = x_open(0, other)
-    y_open(2, 0)
-    y_open(2, 1)
-    y_open(1, 0)
+    a_west, a_east, a_near_east, a_near_west = x_open(0, other)
+    for chunk, d in ((2, 0), (2, 1), (1, 0), (3, 1), (1, 1), (3, 0), (0, 0), (0, 1)):
+        y_open(chunk, d)
     for later, peer in met:
 
         @pl.when(jnp.logical_not(later))
@@ -191,13 +181,29 @@
     loads[1].start()
     loads[2].start()
     loads[0].wait()
-    passed_a = x_pass(0, other, opened_a)
-    y_open(3, 1)
-    opened_b = x_open(1, half)
-    y_open(1, 1)
-    for d in (0, 1):
-        opened_a[2 + d].wait_recv()
-        passed_a[d].wait_recv()
+
+    def pass_on(arrived, slot, start, to, land, term=grad, count=A):
+        arrived.wait_recv()
+        add_into(slot, term, start, count)
+        return copies.send(slot, land, to)
+
+    def x_pass(slot, h, to_east, to_west):
+        one = pass_on(
+            to_east, x_first.at[slot, 1], at_x(1, h, 1).start, east, x_third.at[slot, 1]
+        )
+        two = pass_on(
+            to_west, x_first.at[slot, 0], at_x(3, h, 0).start, west, x_third.at[slot, 0]
+        )
+        return [two, one]
+
+    a_passed = x_pass(0, other, a_east, a_west)
+    q_west = copies.send(y_add(2, 0), q_first.at[0], west)
+    q_east = copies.send(y_add(2, 1), q_first.at[1], east)
+    b_west = copies.send(grad_hbm.at[at_x(2, half, 0)], x_first.at[1, 0], west)
+    b_east = copies.send(grad_hbm.at[at_x(2, half, 1)], x_first.at[1, 1], east)
+    for d, near in ((0, a_near_east), (1, a_near_west)):
+        near.wait_recv()
+        a_passed[d].wait_recv()
         base = at_x(0, other, d).start
 
         def body(i, d=d, base=base):
@@ -207,20 +213,20 @@
             )
 
         over_tiles(A, body)
-        crossed = copies.send(x_sum.at[d], x_from_y.at[d], across)
-        y_copies["x", d] = crossed
-    y_open(3, 0)
-    passed_b = x_pass(1, half, opened_b)
-    y_open(0, 0)
-    y_open(0, 1)
-    q_opened = [
-        copies.send(y_add(2, 0), q_first.at[0], west),
-        copies.send(y_add(2, 1), q_first.at[1], east),
+        y_copies["x", d] = copies.send(x_sum.at[d], x_from_y.at[d], across)
+    q_near = [
         copies.send(y_add(1, 0), q_second.at[0], east),
         copies.send(y_add(3, 1), q_second.at[1], west),
     ]
+    b_near = [
+        copies.send(grad_hbm.at[at_x(1, half, 0)], x_second.at[1, 0], east),
+        copies.send(grad_hbm.at[at_x(3, half, 1)], x_second.at[1, 1], west),
+    ]
     y_add(1, 1)
+    q_on_east = pass_on(q_east, q_first.at[1], 0, east, q_third.at[1], y_sum.at[3], B)
     y_add(3, 0)
+    q_on_west = pass_on(q_west, q_first.at[0], 0, west, q_third.at[0], y_sum.at[6], B)
+    b_passed = x_pass(1, half, b_east, b_west)
 
     squares[...] = jnp.zeros(TILE, jnp.float32)
 
@@ -229,18 +235,19 @@
         mean[at] = value
         squares[...] += jnp.sum(value * value, axis=0)
 
-    for d in (0, 1):
-        opened_b[2 + d].wait_recv()
-        passed_b[d].wait_recv()
-        y_copies["x", d].wait_recv()
-        base = at_x(0, half, d).start
+    for d, passed in ((0, q_on_west), (1, q_on_east)):
+        y_add(0, d)
+        q_near[d].wait_recv()
+        passed.wait_recv()
+        base = at_y(half, 0, d).start
 
         def body(i, d=d, base=base):
             at = pl.ds(i, STEP)
-            own = grad[pl.ds(base + i, STEP)] + x_second[1, d, at] + x_third[1, d, at]
-            store_mean(pl.ds(base + i, STEP), own + x_from_y[d, at])
-
-        over_tiles(A, body)
+            store_mean(
+                pl.ds(base + i, STEP), y_sum[d, at] + q_second[d, at] + q_third[d, at]
+            )
+
+        over_tiles(B, body)
 
     def gather(at, to):
         return copies.send(mean.at[at], mean.at[at], to)
@@ -253,30 +260,35 @@
             gather(at_x(0, h, 0), west),
         ]
 
-    x_crossed = gather(at_x(0, half, 0, 2), across)
-    x_own = x_gather(half)
-
-    q_opened[1].wait_recv()
-    add_into(q_first.at[1], y_sum.at[3], 0, B)
-    q_east = copies.send(q_first.at[1], q_third.at[1], east)
-    q_opened[0].wait_recv()
-    add_into(q_first.at[0], y_sum.at[6], 0, B)
-    q_west = copies.send(q_first.at[0], q_third.at[0], west)
-    q_passed = [q_west, q_east]
+    q_own = [
+        gather(at_y(half, 0, 0), east),
+        gather(at_y(half, 0, 1), west),
+        gather(at_y(half, 0, 1), east),
+        gather(at_y(half, 0, 0), west),
+    ]
+    y_gathered = {}
+
+    def y_gather(chunk, d):
+        y_gathered[chunk, d] = gather(at_y(half, chunk, d), across)
+
+    y_gather(0, 0)
+    y_gather(0, 1)
 
     for d in (0, 1):
-        y_add(0, d)
-        q_opened[2 + d].wait_recv()
-        q_passed[d].wait_recv()
-        base = at_y(half, 0, d).start
+        b_near[d].wait_recv()
+        b_passed[d].wait_recv()
+        y_copies["x", d].wait_recv()
+        base = at_x(0, half, d).start
 
         def body(i, d=d, base=base):
             at = pl.ds(i, STEP)
-            store_mean(
-                pl.ds(base + i, STEP), y_sum[d, at] + q_second[d, at] + q_third[d, at]
-            )
-
-        over_tiles(B, body)
+            own = grad[pl.ds(base + i, STEP)] + x_second[1, d, at] + x_third[1, d, at]
+            store_mean(pl.ds(base + i, STEP), own + x_from_y[d, at])
+
+        over_tiles(A, body)
+
+    x_own = x_gather(half)
+    x_crossed = gather(at_x(0, half, 0, 2), across)
 
     def norm_send(slots, mine, value, to):
         slots[mine] = value
@@ -295,26 +307,6 @@
         pl.semaphore_wait(met_sem, above)
 
     sent = norm_send(norm_z, z, squares[...], z_peers)
-    q_own = [
-        gather(at_y(half, 0, 0), east),
-        gather(at_y(half, 0, 1), west),
-        gather(at_y(half, 0, 1), east),
-        gather(at_y(half, 0, 0), west),
-    ]
-    y_gathered = {}
-
-    def y_gather(chunk, d):
-        y_gathered[chunk, d] = gather(at_y(half, chunk, d), across)
-
-    y_gather(0, 0)
-    y_gather(0, 1)
-
-    x_own[0].wait_recv()
-    x_on = [gather(at_x(3, half, 0), east)]
-    x_own[1].wait_recv()
-    x_on += [gather(at_x(1, half, 1), west)]
-    value = norm_take(norm_z, sent)
-    sent = norm_send(norm_core, core, value, [core_peer])
 
     q_own[0].wait_recv()
     q_on = [gather(at_y(half, 3, 0), east)]
@@ -322,12 +314,18 @@
     q_own[1].wait_recv()
     q_on += [gather(at_y(half, 1, 1), west)]
     y_gather(1, 1)
-    value = norm_take(norm_core, sent)
-    sent = norm_send(norm_x, x, value, x_peers)
+    value = norm_take(norm_z, sent)
+    sent = norm_send(norm_core, core, value, [core_peer])
     q_own[2].wait_recv()
     y_gather(3, 1)
     q_own[3].wait_recv()
     y_gather(1, 0)
+    value = norm_take(norm_core, sent)
+    sent = norm_send(norm_x, x, value, x_peers)
+    x_own[0].wait_recv()
+    x_on = [gather(at_x(3, half, 0), east)]
+    x_own[1].wait_recv()
+    x_on += [gather(at_x(1, half, 1), west)]
     x_crossed.wait_recv()
     x_far = x_gather(other)
     value = norm_take(norm_x, sent)

time: 67.4 us -> 65.3 us (0.969)
  Pallas kernels: 66.6 us -> 64.6 us
    pallas_call x1, Pallas kernels: 63.3 us -> 61.2 us  [per_device(): pl.pallas_call(functools.partial(kernel, entries), out_shape=[near, near]...]
where the time goes in v3:
time: 65.3 us; the launch traced here: 65.2 us
  Pallas kernels  64.6 us (99%)
    pallas_call x1, Pallas kernels, per_device(): pl.pallas_call(functools.partial(kernel, entries), out_shape=[near, near]...  61.2 us
    pallas_call x1, Pallas kernels, per_device(): pl.pallas_call(store_kernel, out_shape=[far, far], in_specs=[pl.BlockSpec...  3.37 us

profile of v3, /device:TPU:0, one launch (start us, length us, event | category | flops | bytes accessed | tf_op | source)
XLA Modules:
  0.0 65.2 jit_solution(4141659480469272998)
XLA Ops:
  0.6 61.2 %outer_step.1 = (f32[1024,8,128]{2,1,0:T(8,128)S(1)}, f32[1024,8,128]{2,1,0:T(8,128)S(1)}) custom-call(f32[1024,8,128]{2,1,0:T(8,128)} %bitcast.25, f32[1024,8,128]{2,1,0:T(8,128)} %bitcast.26, f32[1024,8,128]{2,1,0:T(8,128)} %bitcast.27), custom_call_target="tpu_custom_call" | custom-call | tf_op jit(solution)/shard_map/outer_step/pallas_call | solution.py:421
  61.8 3.4 %store.1 = (f32[1024,8,128]{2,1,0:T(8,128)}, f32[1024,8,128]{2,1,0:T(8,128)}) custom-call(f32[1024,8,128]{2,1,0:T(8,128)S(1)} %get-tuple-element.6.params, f32[1024,8,128]{2,1,0:T(8,128)S(1)} %get-tuple-element.7.momentum), custom_call_target="tpu_custom_call" | custom-call | tf_op jit(solution)/shard_map/store/pallas_call | solution.py:455

commit v4 on v3

v4 whole, which is shorter than its diff:
```python
import functools
import math

import jax
import jax.numpy as jnp
from jax import lax
from jax.experimental import pallas as pl
from jax.experimental.pallas import tpu as pltpu
from jax.sharding import PartitionSpec as P

MESH = pl.DeviceIdType.MESH
TILE = (8, 128)
TILES = 1024
A = 36
B = 28
STEP = 4
FIRST, REST = pl.ds(0, 16), pl.ds(16, A - 16)
GROUPS = 8


def tiles_of(block):
    rows, columns = block.shape
    cut = block.reshape(rows // 8, 8, columns // 128, 128)
    return cut.transpose(0, 2, 1, 3).reshape(-1, 8, 128)


def block_of(tiles, rows, columns):
    cut = tiles.reshape(rows // 8, columns // 128, 8, 128)
    return cut.transpose(0, 2, 1, 3).reshape(rows, columns)


def over_tiles(count, body):
    def step(i, carry):
        body(pl.multiple_of(i * STEP, STEP))
        return carry

    lax.fori_loop(0, count // STEP, step, 0)


class Copies:
    def __init__(self, send_sem, recv_sem, any_tiles):
        self.send_sem, self.recv_sem, self.any_tiles = send_sem, recv_sem, any_tiles
        self.groups, self.sent = 0, {}

    def group(self):
        self.groups += 1
        return Group(self, self.recv_sem.at[self.groups - 1])

    def wait(self, tiles, send=None, recv=None):
        some = self.any_tiles.at[pl.ds(0, tiles)]
        copy = pltpu.make_async_remote_copy(
            src_ref=some,
            dst_ref=some,
            send_sem=self.send_sem.at[0] if send is None else send,
            recv_sem=self.recv_sem.at[0] if recv is None else recv,
            device_id=self.anyone,
            device_id_type=MESH,
        )
        if recv is None:
            copy.wait_send()
        else:
            copy.wait_recv()

    def finish(self):
        for number, tiles in self.sent.items():
            self.wait(tiles, send=self.send_sem.at[number])


class Group:
    def __init__(self, copies, sem):
        self.copies, self.sem, self.tiles = copies, sem, 0

    def send(self, src, dst, to):
        number, device = to
        tiles = math.prod(src.shape) // math.prod(TILE)
        pltpu.make_async_remote_copy(
            src_ref=src,
            dst_ref=dst,
            send_sem=self.copies.send_sem.at[number],
            recv_sem=self.sem,
            device_id=device,
            device_id_type=MESH,
        ).start()
        self.tiles += tiles
        self.copies.sent[number] = self.copies.sent.get(number, 0) + tiles

    def wait(self):
        self.copies.wait(self.tiles, recv=self.sem)


GROUPS_OF_COPIES = 33


def kernel(
    entries,
    grad_hbm,
    params_hbm,
    momentum_hbm,
    new_params,
    new_momentum,
    grad,
    params,
    momentum,
    mean,
    x_first,
    x_second,
    x_third,
    x_sum,
    x_from_y,
    y_sum,
    q_first,
    q_second,
    q_third,
    squares,
    norm_z,
    norm_core,
    norm_x,
    norm_y,
    send_sem,
    recv_sem,
    load_sem,
    met_sem,
):
    outer, inner = lax.axis_index("outer"), lax.axis_index("inner")
    x, half = lax.rem(outer, 4), lax.div(outer, 4)
    low, z, core = lax.div(inner, 8), lax.rem(lax.div(inner, 2), 4), lax.rem(inner, 2)
    y = half * 2 + low

    def device(x=x, y=y, z=z, core=core):
        return (lax.div(y, 2) * 4 + x, (lax.rem(y, 2) * 4 + z) * 2 + core)

    def ring(at, by):
        return lax.rem(at + by, 4)

    east, west, across = [
        (0, device(x=ring(x, 1))),
        (1, device(x=ring(x, 3))),
        (2, device(y=ring(y, 2))),
    ]
    x_peers = [(3, device(x=ring(x, k))) for k in (1, 2, 3)]
    y_peers = [(3, device(y=ring(y, k))) for k in (1, 2, 3)]
    z_peers = [(3, device(z=ring(z, k))) for k in (1, 2, 3)]
    core_peer = (3, device(core=1 - core))

    met = [(ring(z, k) > z, device(z=ring(z, k))) for k in (1, 2, 3)]
    met += [(ring(y, k) > y, device(y=ring(y, k))) for k in (1, 3)]
    met += [(core == 0, core_peer[1])]
    above = sum(jnp.where(later, 1, 0) for later, _ in met)

    barrier = pltpu.get_barrier_semaphore()
    group = [east, west, across]
    for _, peer in group:
        pl.semaphore_signal(barrier, inc=1, device_id=peer, device_id_type=MESH)
    for later, peer in met:

        @pl.when(later)
        def greet(peer=peer):
            pl.semaphore_signal(barrier, inc=1, device_id=peer, device_id_type=MESH)

    loads = [
        pltpu.make_async_copy(src, dst, load_sem.at[i])
        for i, (src, dst) in enumerate(
            ((grad_hbm, grad), (params_hbm, params), (momentum_hbm, momentum))
        )
    ]
    loads[0].start()
    pl.semaphore_wait(barrier, len(group) + len(met) - above)

    copies = Copies(send_sem, recv_sem, mean)
    copies.anyone = east[1]
    other = 1 - half

    def at_x(chunk, h, d, pieces=1):
        return pl.ds(((ring(x, chunk) * 2 + h) * 2 + d) * A, pieces * A)

    def at_y(h, chunk, d, pieces=1):
        return pl.ds(16 * A + ((h * 4 + ring(x, chunk)) * 2 + d) * B, pieces * B)

    a_west, a_east, a_rest = copies.group(), copies.group(), copies.group()
    b_west, b_east, b_rest = copies.group(), copies.group(), copies.group()
    q_west, q_east, q_rest = copies.group(), copies.group(), copies.group()
    y_first = {(chunk, d): copies.group() for chunk, d in ((2, 0), (1, 0), (3, 1), (1, 1), (3, 0))}

    def x_open(group, chunk, h, d, land, to, cut=None):
        at = at_x(chunk, h, d)
        if cut is not None:
            at, land = cut_of(at, cut), land.at[cut]
        group.send(grad_hbm.at[at], land, to)

    def y_open(group, chunk, d, pieces=1):
        group.send(
            grad_hbm.at[at_y(other, chunk, d, pieces)],
            y_sum.at[chunk, pl.ds(d * B, pieces * B)],
            across,
        )

    def cut_of(at, cut):
        return pl.ds(at.start + cut.start, cut.size)

    def add_into(ref, term, start, count):
        def body(i):
            ref[pl.ds(i, STEP)] += term[pl.ds(start + i, STEP)]

        over_tiles(count, body)

    def y_add(chunk, d, pieces=1):
        piece = y_sum.at[chunk, pl.ds(d * B, pieces * B)]
        add_into(piece, grad, at_y(half, chunk, d).start, pieces * B)
        return piece

    x_open(a_west, 2, other, 0, x_first.at[0, 0], west)
    x_open(a_east, 2, other, 1, x_first.at[0, 1], east)
    x_open(a_rest, 1, other, 0, x_second.at[0, 0], east)
    x_open(a_rest, 3, other, 1, x_second.at[0, 1], west)
    y_open(y_first[2, 0], 2, 0, 2)
    x_open(b_west, 2, half, 0, x_first.at[1, 0], west)
    x_open(b_east, 2, half, 1, x_first.at[1, 1], east)
    for chunk, d in ((1, 0), (3, 1), (1, 1), (3, 0)):
        y_open(y_first[chunk, d], chunk, d)
    y_open(q_rest, 0, 0, 2)
    for later, peer in met:

        @pl.when(jnp.logical_not(later))
        def answer(peer=peer):
            pl.semaphore_signal(met_sem, inc=1, device_id=peer, device_id_type=MESH)

    loads[1].start()
    loads[2].start()
    loads[0].wait()

    def pass_on(arrived, rest, ref, land, to, term, start, count):
        arrived.wait()
        add_into(ref, term, start, count)
        rest.send(ref, land, to)

    def x_pass(slot, h, from_east, from_west, rest):
        for arrived, d, chunk, to in ((from_west, 1, 1, east), (from_east, 0, 3, west)):
            pass_on(
                arrived,
                rest,
                x_first.at[slot, d],
                x_third.at[slot, d],
                to,
                grad,
                at_x(chunk, h, d).start,
                A,
            )

    x_pass(0, other, a_west, a_east, a_rest)
    y_first[2, 0].wait()
    y_add(2, 0, 2)
    q_west.send(y_sum.at[2, pl.ds(0, B)], q_first.at[0], west)
    q_east.send(y_sum.at[2, pl.ds(B, B)], q_first.at[1], east)
    y_first[1, 0].wait()
    q_rest.send(y_add(1, 0), q_second.at[0], east)
    y_first[3, 1].wait()
    q_rest.send(y_add(3, 1), q_second.at[1], west)
    a_rest.wait()
    for d in (0, 1):
        base = at_x(0, other, d).start

        def body(i, d=d, base=base):
            x_sum[pl.ds(d * A + i, STEP)] = (
                grad[pl.ds(base + i, STEP)]
                + x_second[0, d, pl.ds(i, STEP)]
                + x_third[0, d, pl.ds(i, STEP)]
            )

        over_tiles(A, body)
    b_rest.send(x_sum, x_from_y, across)
    x_open(b_rest, 1, half, 0, x_second.at[1, 0], east, FIRST)
    x_open(b_rest, 3, half, 1, x_second.at[1, 1], west, FIRST)
    y_first[1, 1].wait()
    y_add(1, 1)
    pass_on(q_east, q_rest, q_first.at[1], q_third.at[1], east, y_sum.at[1], B, B)
    y_first[3, 0].wait()
    y_add(3, 0)
    pass_on(q_west, q_rest, q_first.at[0], q_third.at[0], west, y_sum.at[3], 0, B)
    x_open(b_rest, 1, half, 0, x_second.at[1, 0], east, REST)
    x_open(b_rest, 3, half, 1, x_second.at[1, 1], west, REST)
    x_pass(1, half, b_west, b_east, b_rest)

    squares[...] = jnp.zeros(TILE, jnp.float32)

    def store_mean(at, value):
        value = value / jnp.float32(GROUPS)
        mean[at] = value
        squares[...] += jnp.sum(value * value, axis=0)

    q_rest.wait()
    y_add(0, 0, 2)
    for d in (0, 1):
        base = at_y(half, 0, d).start

        def body(i, d=d, base=base):
            at = pl.ds(i, STEP)
            store_mean(
                pl.ds(base + i, STEP),
                y_sum[0, pl.ds(d * B + i, STEP)] + q_second[d, at] + q_third[d, at],
            )

        over_tiles(B, body)

    def gather(group, at, to):
        group.send(mean.at[at], mean.at[at], to)

    q_from_west, q_from_east, q_far = copies.group(), copies.group(), copies.group()
    x_from_west, x_from_east, crossed = copies.group(), copies.group(), copies.group()
    x_cuts = [(cut, copies.group(), copies.group()) for cut in (FIRST, REST)]
    early, late, last_first, last_rest, last_y = [copies.group() for _ in range(5)]

    gather(q_from_west, at_y(half, 0, 0, 2), east)
    gather(q_from_east, at_y(half, 0, 0, 2), west)
    gather(early, at_y(half, 0, 0, 2), across)

    b_rest.wait()
    for d in (0, 1):
        base = at_x(0, half, d).start

        def body(i, d=d, base=base):
            at = pl.ds(i, STEP)
            own = grad[pl.ds(base + i, STEP)] + x_second[1, d, at] + x_third[1, d, at]
            store_mean(pl.ds(base + i, STEP), own + x_from_y[pl.ds(d * A + i, STEP)])

        over_tiles(A, body)

    gather(x_from_west, at_x(0, half, 0), east)
    gather(x_from_east, at_x(0, half, 1), west)
    gather(early, at_x(0, half, 1), east)
    gather(early, at_x(0, half, 0), west)
    gather(crossed, at_x(0, half, 0, 2), across)

    def norm_send(slots, mine, value, to):
        group = copies.group()
        slots[mine] = value
        for peer in to:
            group.send(slots.at[mine], slots.at[mine], peer)
        return group

    def norm_take(slots, group):
        group.wait()
        total = slots[0]
        for i in range(1, slots.shape[0]):
            total = total + slots[i]
        return total

    @pl.when(above > 0)
    def all_met():
        pl.semaphore_wait(met_sem, above)

    sent = norm_send(norm_z, z, squares[...], z_peers)

    q_from_west.wait()
    gather(q_far, at_y(half, 3, 0), east)
    gather(early, at_y(half, 3, 0, 2), across)
    q_from_east.wait()
    gather(q_far, at_y(half, 1, 1), west)
    gather(early, at_y(half, 1, 0, 2), across)
    value = norm_take(norm_z, sent)
    sent = norm_send(norm_core, core, value, [core_peer])
    value = norm_take(norm_core, sent)
    sent = norm_send(norm_x, x, value, x_peers)
    x_from_west.wait()
    gather(early, at_x(3, half, 0), east)
    x_from_east.wait()
    gather(early, at_x(1, half, 1), west)
    crossed.wait()
    for cut, from_west, from_east in x_cuts:
        gather(from_west, cut_of(at_x(0, other, 0), cut), east)
        gather(from_east, cut_of(at_x(0, other, 1), cut), west)
    gather(late, at_x(0, other, 1), east)
    gather(late, at_x(0, other, 0), west)
    value = norm_take(norm_x, sent)
    sent = norm_send(norm_y, y, value, y_peers)
    q_far.wait()
    gather(last_y, at_y(half, 2, 0, 2), across)
    for (cut, from_west, from_east), last in zip(x_cuts, (last_first, last_rest)):
        from_west.wait()
        gather(last, cut_of(at_x(3, other, 0), cut), east)
        from_east.wait()
        gather(last, cut_of(at_x(1, other, 1), cut), west)
    total = norm_take(norm_y, sent)
    norm = jnp.sqrt(jnp.sum(total, keepdims=True) + 1e-06)
    factor = jnp.broadcast_to(
        jnp.minimum(1.0, 0.5 * math.sqrt(entries) / norm), TILE
    )[None]

    loads[1].wait()
    loads[2].wait()

    def update(at):
        start, count = at.start, at.size

        def body(i):
            at = pl.ds(start + i, STEP)
            clipped = factor * mean[at]
            moved = 0.9 * momentum[at] + clipped
            new_momentum[at] = moved
            new_params[at] = params[at] - 0.7 * (clipped + 0.9 * moved)

        over_tiles(count, body)

    update(at_x(0, half, 0, 2))
    update(at_x(3, half, 0))
    update(at_x(1, half, 1))
    for chunk in range(4):
        update(at_y(half, chunk, 0, 2))
    update(at_x(0, other, 0, 2))
    update(at_x(3, other, 0))
    update(at_x(1, other, 1))
    early.wait()
    update(at_x(3, half, 1))
    update(at_x(1, half, 0))
    update(at_x(2, half, 0, 2))
    for chunk in (0, 3, 1):
        update(at_y(other, chunk, 0, 2))
    late.wait()
    update(at_x(3, other, 1))
    update(at_x(1, other, 0))
    last_first.wait()
    update(cut_of(at_x(2, other, 0), FIRST))
    update(cut_of(at_x(2, other, 1), FIRST))
    last_y.wait()
    update(at_y(other, 2, 0, 2))
    last_rest.wait()
    update(cut_of(at_x(2, other, 0), REST))
    update(cut_of(at_x(2, other, 1), REST))
    copies.finish()
    assert copies.groups == GROUPS_OF_COPIES, copies.groups


def store_kernel(params, momentum, params_out, momentum_out, sem):
    cuts = 1
    size = TILES // cuts
    copies = []
    for i in range(cuts):
        for j, (src, dst) in enumerate(((params, params_out), (momentum, momentum_out))):
            at = pl.ds(i * size, size)
            copy = pltpu.make_async_copy(src.at[at], dst.at[at], sem.at[i * 2 + j])
            copy.start()
            copies.append(copy)
    for copy in copies:
        copy.wait()


def per_device(pseudo_grad, params, momentum):
    rows, columns = params.shape
    entries = rows * lax.axis_size("inner") * columns
    f32 = jnp.float32
    near = pltpu.VMEM((TILES, *TILE), f32)
    far = jax.ShapeDtypeStruct((TILES, *TILE), f32)

    def vmem(*lead):
        return pltpu.VMEM((*lead, *TILE), f32)

    results = pl.pallas_call(
        functools.partial(kernel, entries),
        out_shape=[near, near],
        in_specs=[pl.BlockSpec(memory_space=pl.ANY)] * 3,
        out_specs=[pl.BlockSpec(memory_space=pltpu.VMEM)] * 2,
        scratch_shapes=[
            vmem(TILES),
            vmem(TILES),
            vmem(TILES),
            vmem(TILES),
            vmem(2, 2, A),
            vmem(2, 2, A),
            vmem(2, 2, A),
            vmem(2 * A),
            vmem(2 * A),
            vmem(4, 2 * B),
            vmem(2, B),
            vmem(2, B),
            vmem(2, B),
            vmem(),
            vmem(4),
            vmem(2),
            vmem(4),
            vmem(4),
            pltpu.SemaphoreType.DMA((4,)),
            pltpu.SemaphoreType.DMA((GROUPS_OF_COPIES,)),
            pltpu.SemaphoreType.DMA((3,)),
            pltpu.SemaphoreType.REGULAR,
        ],
        compiler_params=pltpu.CompilerParams(
            collective_id=0, has_side_effects=True, vmem_limit_bytes=49 * 2**20
        ),
        name="outer_step",
    )(tiles_of(pseudo_grad[0]), tiles_of(params), tiles_of(momentum))
    results = pl.pallas_call(
        store_kernel,
        out_shape=[far, far],
        in_specs=[pl.BlockSpec(memory_space=pltpu.VMEM)] * 2,
        out_specs=[pl.BlockSpec(memory_space=pl.ANY)] * 2,
        scratch_shapes=[pltpu.SemaphoreType.DMA((2,))],
        compiler_params=pltpu.CompilerParams(vmem_limit_bytes=40 * 2**20),
        name="store",
    )(*results)
    return tuple(block_of(result, rows, columns) for result in results)


def solution(mesh):
    placed = (P("outer", "inner", None), P("inner", None), P("inner", None))
    return jax.shard_map(
        per_device,
        mesh=mesh,
        in_specs=placed,
        out_specs=(P("inner", None), P("inner", None)),
        check_vma=False,
    )
```

time: 65.3 us -> 64.3 us (0.985)
  Pallas kernels: 64.6 us -> 63.6 us
    pallas_call x1, Pallas kernels: 61.2 us -> 60.1 us  [per_device(): pl.pallas_call(functools.partial(kernel, entries), out_shape=[near, near]...]
where the time goes in v4:
time: 64.3 us; the launch traced here: 64.2 us
  Pallas kernels  63.6 us (99%)
    pallas_call x1, Pallas kernels, per_device(): pl.pallas_call(functools.partial(kernel, entries), out_shape=[near, near]...  60.1 us
    pallas_call x1, Pallas kernels, per_device(): pl.pallas_call(store_kernel, out_shape=[far, far], in_specs=[pl.BlockSpec...  3.41 us

profile of v4, /device:TPU:0, one launch (start us, length us, event | category | flops | bytes accessed | tf_op | source)
XLA Modules:
  0.0 64.2 jit_solution(14929212213050900091)
XLA Ops:
  0.6 60.1 %outer_step.1 = (f32[1024,8,128]{2,1,0:T(8,128)S(1)}, f32[1024,8,128]{2,1,0:T(8,128)S(1)}) custom-call(f32[1024,8,128]{2,1,0:T(8,128)} %bitcast.25, f32[1024,8,128]{2,1,0:T(8,128)} %bitcast.26, f32[1024,8,128]{2,1,0:T(8,128)} %bitcast.27), custom_call_target="tpu_custom_call" | custom-call | tf_op jit(solution)/shard_map/outer_step/pallas_call | solution.py:456
  60.8 3.4 %store.1 = (f32[1024,8,128]{2,1,0:T(8,128)}, f32[1024,8,128]{2,1,0:T(8,128)}) custom-call(f32[1024,8,128]{2,1,0:T(8,128)S(1)} %get-tuple-element.6.params, f32[1024,8,128]{2,1,0:T(8,128)S(1)} %get-tuple-element.7.momentum), custom_call_target="tpu_custom_call" | custom-call | tf_op jit(solution)/shard_map/store/pallas_call | solution.py:490

commit v5 on v4

--- a/solution.py
+++ b/solution.py
@@ -119,6 +119,9 @@
     send_sem,
     recv_sem,
     load_sem,
+    west_sem,
+    east_sem,
+    across_sem,
     met_sem,
 ):
     outer, inner = lax.axis_index("outer"), lax.axis_index("inner")
@@ -142,18 +145,21 @@
     z_peers = [(3, device(z=ring(z, k))) for k in (1, 2, 3)]
     core_peer = (3, device(core=1 - core))
 
-    met = [(ring(z, k) > z, device(z=ring(z, k))) for k in (1, 2, 3)]
-    met += [(ring(y, k) > y, device(y=ring(y, k))) for k in (1, 3)]
-    met += [(core == 0, core_peer[1])]
-    above = sum(jnp.where(later, 1, 0) for later, _ in met)
+    met = [
+        (ring(x, 3) > x, west, west_sem, east_sem),
+        (ring(x, 1) > x, east, east_sem, west_sem),
+        (half == 0, across, across_sem, across_sem),
+    ]
+    met += [(ring(y, k) > y, (3, device(y=ring(y, k))), met_sem, met_sem) for k in (1, 3)]
+    met += [(core == 1, core_peer, met_sem, met_sem)]
+    met += [(ring(z, k) > z, (3, device(z=ring(z, k))), met_sem, met_sem) for k in (1, 2, 3)]
+    lower = sum(jnp.where(higher, 0, 1) for higher, *_ in met)
+    above = sum(jnp.where(higher, 1, 0) for higher, *_ in met[3:])
 
     barrier = pltpu.get_barrier_semaphore()
-    group = [east, west, across]
-    for _, peer in group:
-        pl.semaphore_signal(barrier, inc=1, device_id=peer, device_id_type=MESH)
-    for later, peer in met:
-
-        @pl.when(later)
+    for higher, (_, peer), _, _ in met:
+
+        @pl.when(higher)
         def greet(peer=peer):
             pl.semaphore_signal(barrier, inc=1, device_id=peer, device_id_type=MESH)
 
@@ -164,7 +170,23 @@
         )
     ]
     loads[0].start()
-    pl.semaphore_wait(barrier, len(group) + len(met) - above)
+
+    @pl.when(lower > 0)
+    def all_lower():
+        pl.semaphore_wait(barrier, lower)
+
+    def answer(higher, peer, _, theirs):
+        @pl.when(jnp.logical_not(higher))
+        def signal():
+            pl.semaphore_signal(theirs, inc=1, device_id=peer[1], device_id_type=MESH)
+
+    def answered(higher, _, mine, __):
+        @pl.when(higher)
+        def wait():
+            pl.semaphore_wait(mine, 1)
+
+    for entry in met[:3]:
+        answer(*entry)
 
     copies = Copies(send_sem, recv_sem, mean)
     copies.anyone = east[1]
@@ -208,21 +230,38 @@
         add_into(piece, grad, at_y(half, chunk, d).start, pieces * B)
         return piece
 
+    def y_open_all():
+        y_open(y_first[2, 0], 2, 0, 2)
+        for chunk, d in ((1, 0), (3, 1), (1, 1), (3, 0)):
+            y_open(y_first[chunk, d], chunk, d)
+        y_open(q_rest, 0, 0, 2)
+
+    counts = copies.sent.get(2, 0), {g: g.tiles for g in (*y_first.values(), q_rest)}
+
+    @pl.when(half == 1)
+    def y_now():
+        y_open_all()
+
+    copies.sent[2] = counts[0]
+    for group, tiles in counts[1].items():
+        group.tiles = tiles
+
+    answered(*met[0])
     x_open(a_west, 2, other, 0, x_first.at[0, 0], west)
+    x_open(a_rest, 3, other, 1, x_second.at[0, 1], west)
+    x_open(b_west, 2, half, 0, x_first.at[1, 0], west)
+    answered(*met[1])
     x_open(a_east, 2, other, 1, x_first.at[0, 1], east)
     x_open(a_rest, 1, other, 0, x_second.at[0, 0], east)
-    x_open(a_rest, 3, other, 1, x_second.at[0, 1], west)
-    y_open(y_first[2, 0], 2, 0, 2)
-    x_open(b_west, 2, half, 0, x_first.at[1, 0], west)
     x_open(b_east, 2, half, 1, x_first.at[1, 1], east)
-    for chunk, d in ((1, 0), (3, 1), (1, 1), (3, 0)):
-        y_open(y_first[chunk, d], chunk, d)
-    y_open(q_rest, 0, 0, 2)
-    for later, peer in met:
-
-        @pl.when(jnp.logical_not(later))
-        def answer(peer=peer):
-            pl.semaphore_signal(met_sem, inc=1, device_id=peer, device_id_type=MESH)
+
+    @pl.when(half == 0)
+    def y_answered():
+        pl.semaphore_wait(across_sem, 1)
+        y_open_all()
+
+    for entry in met[3:]:
+        answer(*entry)
 
     loads[1].start()
     loads[2].start()
@@ -481,6 +520,9 @@
             pltpu.SemaphoreType.DMA((GROUPS_OF_COPIES,)),
             pltpu.SemaphoreType.DMA((3,)),
             pltpu.SemaphoreType.REGULAR,
+            pltpu.SemaphoreType.REGULAR,
+            pltpu.SemaphoreType.REGULAR,
+            pltpu.SemaphoreType.REGULAR,
         ],
         compiler_params=pltpu.CompilerParams(
             collective_id=0, has_side_effects=True, vmem_limit_bytes=49 * 2**20

time: 64.3 us -> 62.8 us (0.977)
  Pallas kernels: 63.6 us -> 62.1 us
    pallas_call x1, Pallas kernels: 60.1 us -> 58.7 us  [per_device(): pl.pallas_call(functools.partial(kernel, entries), out_shape=[near, near]...]
where the time goes in v5:
time: 62.8 us; the launch traced here: 62.7 us
  Pallas kernels  62.1 us (99%)
  between operations  0.64 us (1%)
    pallas_call x1, Pallas kernels, per_device(): pl.pallas_call(functools.partial(kernel, entries), out_shape=[near, near]...  58.7 us
    pallas_call x1, Pallas kernels, per_device(): pl.pallas_call(store_kernel, out_shape=[far, far], in_specs=[pl.BlockSpec...  3.41 us

profile of v5, /device:TPU:0, one launch (start us, length us, event | category | flops | bytes accessed | tf_op | source)
XLA Modules:
  0.0 62.7 jit_solution(14813499050776104995)
XLA Ops:
  0.6 58.7 %outer_step.1 = (f32[1024,8,128]{2,1,0:T(8,128)S(1)}, f32[1024,8,128]{2,1,0:T(8,128)S(1)}) custom-call(f32[1024,8,128]{2,1,0:T(8,128)} %bitcast.25, f32[1024,8,128]{2,1,0:T(8,128)} %bitcast.26, f32[1024,8,128]{2,1,0:T(8,128)} %bitcast.27), custom_call_target="tpu_custom_call" | custom-call | tf_op jit(solution)/shard_map/outer_step/pallas_call | solution.py:495
  59.3 3.4 %store.1 = (f32[1024,8,128]{2,1,0:T(8,128)}, f32[1024,8,128]{2,1,0:T(8,128)}) custom-call(f32[1024,8,128]{2,1,0:T(8,128)S(1)} %get-tuple-element.6.params, f32[1024,8,128]{2,1,0:T(8,128)S(1)} %get-tuple-element.7.momentum), custom_call_target="tpu_custom_call" | custom-call | tf_op jit(solution)/shard_map/store/pallas_call | solution.py:532

commit v6 on v5

--- a/solution.py
+++ b/solution.py
@@ -13,7 +13,7 @@
 TILES = 1024
 A = 36
 B = 28
-STEP = 4
+STEP = 10
 FIRST, REST = pl.ds(0, 16), pl.ds(16, A - 16)
 GROUPS = 8
 
@@ -30,11 +30,18 @@
 
 
 def over_tiles(count, body):
-    def step(i, carry):
-        body(pl.multiple_of(i * STEP, STEP))
-        return carry
-
-    lax.fori_loop(0, count // STEP, step, 0)
+    steps, rest = divmod(count, STEP)
+    if steps == 1:
+        body(0, STEP)
+    elif steps > 1:
+
+        def step(i, carry):
+            body(i * STEP, STEP)
+            return carry
+
+        lax.fori_loop(0, steps, step, 0)
+    if rest:
+        body(steps * STEP, rest)
 
 
 class Copies:
@@ -220,8 +227,8 @@
         return pl.ds(at.start + cut.start, cut.size)
 
     def add_into(ref, term, start, count):
-        def body(i):
-            ref[pl.ds(i, STEP)] += term[pl.ds(start + i, STEP)]
+        def body(i, n):
+            ref[pl.ds(i, n)] += term[pl.ds(start + i, n)]
 
         over_tiles(count, body)
 
@@ -246,14 +253,14 @@
     for group, tiles in counts[1].items():
         group.tiles = tiles
 
+    answered(*met[1])
+    x_open(a_east, 2, other, 1, x_first.at[0, 1], east)
+    x_open(a_rest, 1, other, 0, x_second.at[0, 0], east)
+    x_open(b_east, 2, half, 1, x_first.at[1, 1], east)
     answered(*met[0])
     x_open(a_west, 2, other, 0, x_first.at[0, 0], west)
     x_open(a_rest, 3, other, 1, x_second.at[0, 1], west)
     x_open(b_west, 2, half, 0, x_first.at[1, 0], west)
-    answered(*met[1])
-    x_open(a_east, 2, other, 1, x_first.at[0, 1], east)
-    x_open(a_rest, 1, other, 0, x_second.at[0, 0], east)
-    x_open(b_east, 2, half, 1, x_first.at[1, 1], east)
 
     @pl.when(half == 0)
     def y_answered():
@@ -298,11 +305,11 @@
     for d in (0, 1):
         base = at_x(0, other, d).start
 
-        def body(i, d=d, base=base):
-            x_sum[pl.ds(d * A + i, STEP)] = (
-                grad[pl.ds(base + i, STEP)]
-                + x_second[0, d, pl.ds(i, STEP)]
-                + x_third[0, d, pl.ds(i, STEP)]
+        def body(i, n, d=d, base=base):
+            x_sum[pl.ds(d * A + i, n)] = (
+                grad[pl.ds(base + i, n)]
+                + x_second[0, d, pl.ds(i, n)]
+                + x_third[0, d, pl.ds(i, n)]
             )
 
         over_tiles(A, body)
@@ -331,11 +338,11 @@
     for d in (0, 1):
         base = at_y(half, 0, d).start
 
-        def body(i, d=d, base=base):
-            at = pl.ds(i, STEP)
+        def body(i, n, d=d, base=base):
+            at = pl.ds(i, n)
             store_mean(
-                pl.ds(base + i, STEP),
-                y_sum[0, pl.ds(d * B + i, STEP)] + q_second[d, at] + q_third[d, at],
+                pl.ds(base + i, n),
+                y_sum[0, pl.ds(d * B + i, n)] + q_second[d, at] + q_third[d, at],
             )
 
         over_tiles(B, body)
@@ -356,10 +363,10 @@
     for d in (0, 1):
         base = at_x(0, half, d).start
 
-        def body(i, d=d, base=base):
-            at = pl.ds(i, STEP)
-            own = grad[pl.ds(base + i, STEP)] + x_second[1, d, at] + x_third[1, d, at]
-            store_mean(pl.ds(base + i, STEP), own + x_from_y[pl.ds(d * A + i, STEP)])
+        def body(i, n, d=d, base=base):
+            at = pl.ds(i, n)
+            own = grad[pl.ds(base + i, n)] + x_second[1, d, at] + x_third[1, d, at]
+            store_mean(pl.ds(base + i, n), own + x_from_y[pl.ds(d * A + i, n)])
 
         over_tiles(A, body)
 
@@ -430,8 +437,8 @@
     def update(at):
         start, count = at.start, at.size
 
-        def body(i):
-            at = pl.ds(start + i, STEP)
+        def body(i, n):
+            at = pl.ds(start + i, n)
             clipped = factor * mean[at]
             moved = 0.9 * momentum[at] + clipped
             new_momentum[at] = moved

time: 62.8 us -> 62.4 us (level)
  Pallas kernels: 62.1 us -> 61.1 us
    pallas_call x1, Pallas kernels: 58.7 us -> 57.7 us  [per_device(): pl.pallas_call(functools.partial(kernel, entries), out_shape=[near, near]...]
where the time goes in v6:
time: 62.4 us; the launch traced here: 61.8 us
  Pallas kernels  61.1 us (98%)
  between operations  0.64 us (1%)
    pallas_call x1, Pallas kernels, per_device(): pl.pallas_call(functools.partial(kernel, entries), out_shape=[near, near]...  57.7 us
    pallas_call x1, Pallas kernels, per_device(): pl.pallas_call(store_kernel, out_shape=[far, far], in_specs=[pl.BlockSpec...  3.41 us

profile of v6, /device:TPU:0, one launch (start us, length us, event | category | flops | bytes accessed | tf_op | source)
XLA Modules:
  0.0 61.8 jit_solution(14296266608640344822)
XLA Ops:
  0.6 57.7 %outer_step.1 = (f32[1024,8,128]{2,1,0:T(8,128)S(1)}, f32[1024,8,128]{2,1,0:T(8,128)S(1)}) custom-call(f32[1024,8,128]{2,1,0:T(8,128)} %bitcast.25, f32[1024,8,128]{2,1,0:T(8,128)} %bitcast.26, f32[1024,8,128]{2,1,0:T(8,128)} %bitcast.27), custom_call_target="tpu_custom_call" | custom-call | tf_op jit(solution)/shard_map/outer_step/pallas_call | solution.py:502
  58.4 3.4 %store.1 = (f32[1024,8,128]{2,1,0:T(8,128)}, f32[1024,8,128]{2,1,0:T(8,128)}) custom-call(f32[1024,8,128]{2,1,0:T(8,128)S(1)} %get-tuple-element.6.params, f32[1024,8,128]{2,1,0:T(8,128)S(1)} %get-tuple-element.7.momentum), custom_call_target="tpu_custom_call" | custom-call | tf_op jit(solution)/shard_map/store/pallas_call | solution.py:539

commit v7 on v6

--- a/solution.py
+++ b/solution.py
@@ -157,7 +157,7 @@
         (ring(x, 1) > x, east, east_sem, west_sem),
         (half == 0, across, across_sem, across_sem),
     ]
-    met += [(ring(y, k) > y, (3, device(y=ring(y, k))), met_sem, met_sem) for k in (1, 3)]
+    met += [(half == 0, (3, device(y=3 - y)), met_sem, met_sem)]
     met += [(core == 1, core_peer, met_sem, met_sem)]
     met += [(ring(z, k) > z, (3, device(z=ring(z, k))), met_sem, met_sem) for k in (1, 2, 3)]
     lower = sum(jnp.where(higher, 0, 1) for higher, *_ in met)
@@ -313,6 +313,10 @@
             )
 
         over_tiles(A, body)
+    @pl.when(above > 0)
+    def all_met():
+        pl.semaphore_wait(met_sem, above)
+
     b_rest.send(x_sum, x_from_y, across)
     x_open(b_rest, 1, half, 0, x_second.at[1, 0], east, FIRST)
     x_open(b_rest, 3, half, 1, x_second.at[1, 1], west, FIRST)
@@ -389,10 +393,6 @@
         for i in range(1, slots.shape[0]):
             total = total + slots[i]
         return total
-
-    @pl.when(above > 0)
-    def all_met():
-        pl.semaphore_wait(met_sem, above)
 
     sent = norm_send(norm_z, z, squares[...], z_peers)
 

time: 62.4 us -> 62.4 us (level)
  no operation moved by 1% of the time
where the time goes in v7:
time: 62.4 us; the launch traced here: 61.8 us
  Pallas kernels  61.1 us (98%)
  between operations  0.64 us (1%)
    pallas_call x1, Pallas kernels, per_device(): pl.pallas_call(functools.partial(kernel, entries), out_shape=[near, near]...  57.7 us
    pallas_call x1, Pallas kernels, per_device(): pl.pallas_call(store_kernel, out_shape=[far, far], in_specs=[pl.BlockSpec...  3.41 us

profile of v7, /device:TPU:0, one launch (start us, length us, event | category | flops | bytes accessed | tf_op | source)
XLA Modules:
  0.0 61.8 jit_solution(11182946270109472015)
XLA Ops:
  0.6 57.7 %outer_step.1 = (f32[1024,8,128]{2,1,0:T(8,128)S(1)}, f32[1024,8,128]{2,1,0:T(8,128)S(1)}) custom-call(f32[1024,8,128]{2,1,0:T(8,128)} %bitcast.25, f32[1024,8,128]{2,1,0:T(8,128)} %bitcast.26, f32[1024,8,128]{2,1,0:T(8,128)} %bitcast.27), custom_call_target="tpu_custom_call" | custom-call | tf_op jit(solution)/shard_map/outer_step/pallas_call | solution.py:502
  58.4 3.4 %store.1 = (f32[1024,8,128]{2,1,0:T(8,128)}, f32[1024,8,128]{2,1,0:T(8,128)}) custom-call(f32[1024,8,128]{2,1,0:T(8,128)S(1)} %get-tuple-element.6.params, f32[1024,8,128]{2,1,0:T(8,128)S(1)} %get-tuple-element.7.momentum), custom_call_target="tpu_custom_call" | custom-call | tf_op jit(solution)/shard_map/store/pallas_call | solution.py:539

commit v8 on v7

--- a/solution.py
+++ b/solution.py
@@ -280,7 +280,7 @@
         rest.send(ref, land, to)
 
     def x_pass(slot, h, from_east, from_west, rest):
-        for arrived, d, chunk, to in ((from_west, 1, 1, east), (from_east, 0, 3, west)):
+        for arrived, d, chunk, to in ((from_east, 0, 3, west), (from_west, 1, 1, east)):
             pass_on(
                 arrived,
                 rest,

time: 62.4 us -> 62.4 us (level)
  no operation moved by 1% of the time
where the time goes in v8:
time: 62.4 us; the launch traced here: 61.8 us
  Pallas kernels  61.1 us (98%)
  between operations  0.64 us (1%)
    pallas_call x1, Pallas kernels, per_device(): pl.pallas_call(functools.partial(kernel, entries), out_shape=[near, near]...  57.7 us
    pallas_call x1, Pallas kernels, per_device(): pl.pallas_call(store_kernel, out_shape=[far, far], in_specs=[pl.BlockSpec...  3.41 us

profile of v8, /device:TPU:0, one launch (start us, length us, event | category | flops | bytes accessed | tf_op | source)
XLA Modules:
  0.0 61.8 jit_solution(15556798204190972116)
XLA Ops:
  0.6 57.7 %outer_step.1 = (f32[1024,8,128]{2,1,0:T(8,128)S(1)}, f32[1024,8,128]{2,1,0:T(8,128)S(1)}) custom-call(f32[1024,8,128]{2,1,0:T(8,128)} %bitcast.25, f32[1024,8,128]{2,1,0:T(8,128)} %bitcast.26, f32[1024,8,128]{2,1,0:T(8,128)} %bitcast.27), custom_call_target="tpu_custom_call" | custom-call | tf_op jit(solution)/shard_map/outer_step/pallas_call | solution.py:502
  58.4 3.4 %store.1 = (f32[1024,8,128]{2,1,0:T(8,128)}, f32[1024,8,128]{2,1,0:T(8,128)}) custom-call(f32[1024,8,128]{2,1,0:T(8,128)S(1)} %get-tuple-element.6.params, f32[1024,8,128]{2,1,0:T(8,128)S(1)} %get-tuple-element.7.momentum), custom_call_target="tpu_custom_call" | custom-call | tf_op jit(solution)/shard_map/store/pallas_call | solution.py:539

commit v9 on v8

--- a/solution.py
+++ b/solution.py
@@ -13,7 +13,7 @@
 TILES = 1024
 A = 36
 B = 28
-STEP = 10
+STEP = 9
 FIRST, REST = pl.ds(0, 16), pl.ds(16, A - 16)
 GROUPS = 8
 
@@ -147,19 +147,19 @@
         (1, device(x=ring(x, 3))),
         (2, device(y=ring(y, 2))),
     ]
-    x_peers = [(3, device(x=ring(x, k))) for k in (1, 2, 3)]
-    y_peers = [(3, device(y=ring(y, k))) for k in (1, 2, 3)]
-    z_peers = [(3, device(z=ring(z, k))) for k in (1, 2, 3)]
-    core_peer = (3, device(core=1 - core))
+    x_peers = [(2, device(x=ring(x, k))) for k in (1, 2, 3)]
+    y_peers = [(2, device(y=ring(y, k))) for k in (1, 2, 3)]
+    z_peers = [(2, device(z=ring(z, k))) for k in (1, 2, 3)]
+    core_peer = (2, device(core=1 - core))
 
     met = [
         (ring(x, 3) > x, west, west_sem, east_sem),
         (ring(x, 1) > x, east, east_sem, west_sem),
         (half == 0, across, across_sem, across_sem),
     ]
-    met += [(half == 0, (3, device(y=3 - y)), met_sem, met_sem)]
+    met += [(half == 0, (2, device(y=3 - y)), met_sem, met_sem)]
     met += [(core == 1, core_peer, met_sem, met_sem)]
-    met += [(ring(z, k) > z, (3, device(z=ring(z, k))), met_sem, met_sem) for k in (1, 2, 3)]
+    met += [(ring(z, k) > z, (2, device(z=ring(z, k))), met_sem, met_sem) for k in (1, 2, 3)]
     lower = sum(jnp.where(higher, 0, 1) for higher, *_ in met)
     above = sum(jnp.where(higher, 1, 0) for higher, *_ in met[3:])
 
@@ -523,7 +523,7 @@
             vmem(2),
             vmem(4),
             vmem(4),
-            pltpu.SemaphoreType.DMA((4,)),
+            pltpu.SemaphoreType.DMA((3,)),
             pltpu.SemaphoreType.DMA((GROUPS_OF_COPIES,)),
             pltpu.SemaphoreType.DMA((3,)),
             pltpu.SemaphoreType.REGULAR,

time: 62.4 us -> 62.4 us (level)
  no operation moved by 1% of the time
where the time goes in v9:
time: 62.4 us; the launch traced here: 61.8 us
  Pallas kernels  61.1 us (98%)
  between operations  0.64 us (1%)
    pallas_call x1, Pallas kernels, per_device(): pl.pallas_call(functools.partial(kernel, entries), out_shape=[near, near]...  57.7 us
    pallas_call x1, Pallas kernels, per_device(): pl.pallas_call(store_kernel, out_shape=[far, far], in_specs=[pl.BlockSpec...  3.41 us

profile of v9, /device:TPU:0, one launch (start us, length us, event | category | flops | bytes accessed | tf_op | source)
XLA Modules:
  0.0 61.8 jit_solution(3392207909914466239)
XLA Ops:
  0.6 57.7 %outer_step.1 = (f32[1024,8,128]{2,1,0:T(8,128)S(1)}, f32[1024,8,128]{2,1,0:T(8,128)S(1)}) custom-call(f32[1024,8,128]{2,1,0:T(8,128)} %bitcast.25, f32[1024,8,128]{2,1,0:T(8,128)} %bitcast.26, f32[1024,8,128]{2,1,0:T(8,128)} %bitcast.27), custom_call_target="tpu_custom_call" | custom-call | tf_op jit(solution)/shard_map/outer_step/pallas_call | solution.py:502
  58.4 3.4 %store.1 = (f32[1024,8,128]{2,1,0:T(8,128)}, f32[1024,8,128]{2,1,0:T(8,128)}) custom-call(f32[1024,8,128]{2,1,0:T(8,128)S(1)} %get-tuple-element.6.params, f32[1024,8,128]{2,1,0:T(8,128)S(1)} %get-tuple-element.7.momentum), custom_call_target="tpu_custom_call" | custom-call | tf_op jit(solution)/shard_map/store/pallas_call | solution.py:539

commit v10 on v9

--- a/solution.py
+++ b/solution.py
@@ -13,7 +13,7 @@
 TILES = 1024
 A = 36
 B = 28
-STEP = 9
+STEP = 10
 FIRST, REST = pl.ds(0, 16), pl.ds(16, A - 16)
 GROUPS = 8
 
@@ -95,7 +95,7 @@
         self.copies.wait(self.tiles, recv=self.sem)
 
 
-GROUPS_OF_COPIES = 33
+GROUPS_OF_COPIES = 30
 
 
 def kernel(
@@ -205,9 +205,7 @@
     def at_y(h, chunk, d, pieces=1):
         return pl.ds(16 * A + ((h * 4 + ring(x, chunk)) * 2 + d) * B, pieces * B)
 
-    a_west, a_east, a_rest = copies.group(), copies.group(), copies.group()
-    b_west, b_east, b_rest = copies.group(), copies.group(), copies.group()
-    q_west, q_east, q_rest = copies.group(), copies.group(), copies.group()
+    a_both, a_rest, b_both, b_rest, q_both, q_rest = [copies.group() for _ in range(6)]
     y_first = {(chunk, d): copies.group() for chunk, d in ((2, 0), (1, 0), (3, 1), (1, 1), (3, 0))}
 
     def x_open(group, chunk, h, d, land, to, cut=None):
@@ -254,13 +252,13 @@
         group.tiles = tiles
 
     answered(*met[1])
-    x_open(a_east, 2, other, 1, x_first.at[0, 1], east)
+    x_open(a_both, 2, other, 1, x_first.at[0, 1], east)
     x_open(a_rest, 1, other, 0, x_second.at[0, 0], east)
-    x_open(b_east, 2, half, 1, x_first.at[1, 1], east)
+    x_open(b_both, 2, half, 1, x_first.at[1, 1], east)
     answered(*met[0])
-    x_open(a_west, 2, other, 0, x_first.at[0, 0], west)
+    x_open(a_both, 2, other, 0, x_first.at[0, 0], west)
     x_open(a_rest, 3, other, 1, x_second.at[0, 1], west)
-    x_open(b_west, 2, half, 0, x_first.at[1, 0], west)
+    x_open(b_both, 2, half, 0, x_first.at[1, 0], west)
 
     @pl.when(half == 0)
     def y_answered():
@@ -274,15 +272,14 @@
     loads[2].start()
     loads[0].wait()
 
-    def pass_on(arrived, rest, ref, land, to, term, start, count):
-        arrived.wait()
+    def pass_on(rest, ref, land, to, term, start, count):
         add_into(ref, term, start, count)
         rest.send(ref, land, to)
 
-    def x_pass(slot, h, from_east, from_west, rest):
-        for arrived, d, chunk, to in ((from_east, 0, 3, west), (from_west, 1, 1, east)):
+    def x_pass(slot, h, both, rest):
+        both.wait()
+        for d, chunk, to in ((0, 3, west), (1, 1, east)):
             pass_on(
-                arrived,
                 rest,
                 x_first.at[slot, d],
                 x_third.at[slot, d],
@@ -292,11 +289,11 @@
                 A,
             )
 
-    x_pass(0, other, a_west, a_east, a_rest)
+    x_pass(0, other, a_both, a_rest)
     y_first[2, 0].wait()
     y_add(2, 0, 2)
-    q_west.send(y_sum.at[2, pl.ds(0, B)], q_first.at[0], west)
-    q_east.send(y_sum.at[2, pl.ds(B, B)], q_first.at[1], east)
+    q_both.send(y_sum.at[2, pl.ds(0, B)], q_first.at[0], west)
+    q_both.send(y_sum.at[2, pl.ds(B, B)], q_first.at[1], east)
     y_first[1, 0].wait()
     q_rest.send(y_add(1, 0), q_second.at[0], east)
     y_first[3, 1].wait()
@@ -322,13 +319,14 @@
     x_open(b_rest, 3, half, 1, x_second.at[1, 1], west, FIRST)
     y_first[1, 1].wait()
     y_add(1, 1)
-    pass_on(q_east, q_rest, q_first.at[1], q_third.at[1], east, y_sum.at[1], B, B)
+    q_both.wait()
+    pass_on(q_rest, q_first.at[1], q_third.at[1], east, y_sum.at[1], B, B)
     y_first[3, 0].wait()
     y_add(3, 0)
-    pass_on(q_west, q_rest, q_first.at[0], q_third.at[0], west, y_sum.at[3], 0, B)
+    pass_on(q_rest, q_first.at[0], q_third.at[0], west, y_sum.at[3], 0, B)
     x_open(b_rest, 1, half, 0, x_second.at[1, 0], east, REST)
     x_open(b_rest, 3, half, 1, x_second.at[1, 1], west, REST)
-    x_pass(1, half, b_west, b_east, b_rest)
+    x_pass(1, half, b_both, b_rest)
 
     squares[...] = jnp.zeros(TILE, jnp.float32)
 

time: 62.4 us -> 62.4 us (level)
  no operation moved by 1% of the time
where the time goes in v10:
time: 62.4 us; the launch traced here: 61.7 us
  Pallas kernels  61.1 us (98%)
  between operations  0.64 us (1%)
    pallas_call x1, Pallas kernels, per_device(): pl.pallas_call(functools.partial(kernel, entries), out_shape=[near, near]...  57.7 us
    pallas_call x1, Pallas kernels, per_device(): pl.pallas_call(store_kernel, out_shape=[far, far], in_specs=[pl.BlockSpec...  3.41 us

profile of v10, /device:TPU:0, one launch (start us, length us, event | category | flops | bytes accessed | tf_op | source)
XLA Modules:
  0.0 61.7 jit_solution(15374515423192732232)
XLA Ops:
  0.6 57.7 %outer_step.1 = (f32[1024,8,128]{2,1,0:T(8,128)S(1)}, f32[1024,8,128]{2,1,0:T(8,128)S(1)}) custom-call(f32[1024,8,128]{2,1,0:T(8,128)} %bitcast.25, f32[1024,8,128]{2,1,0:T(8,128)} %bitcast.26, f32[1024,8,128]{2,1,0:T(8,128)} %bitcast.27), custom_call_target="tpu_custom_call" | custom-call | tf_op jit(solution)/shard_map/outer_step/pallas_call | solution.py:500
  58.3 3.4 %store.1 = (f32[1024,8,128]{2,1,0:T(8,128)}, f32[1024,8,128]{2,1,0:T(8,128)}) custom-call(f32[1024,8,128]{2,1,0:T(8,128)S(1)} %get-tuple-element.6.params, f32[1024,8,128]{2,1,0:T(8,128)S(1)} %get-tuple-element.7.momentum), custom_call_target="tpu_custom_call" | custom-call | tf_op jit(solution)/shard_map/store/pallas_call | solution.py:537

commit v11 on v8

--- a/solution.py
+++ b/solution.py
@@ -13,7 +13,7 @@
 TILES = 1024
 A = 36
 B = 28
-STEP = 10
+STEP = 9
 FIRST, REST = pl.ds(0, 16), pl.ds(16, A - 16)
 GROUPS = 8
 

time: 62.4 us -> 62.4 us (level)
  no operation moved by 1% of the time
where the time goes in v11:
time: 62.4 us; the launch traced here: 61.8 us
  Pallas kernels  61.1 us (98%)
  between operations  0.64 us (1%)
    pallas_call x1, Pallas kernels, per_device(): pl.pallas_call(functools.partial(kernel, entries), out_shape=[near, near]...  57.7 us
    pallas_call x1, Pallas kernels, per_device(): pl.pallas_call(store_kernel, out_shape=[far, far], in_specs=[pl.BlockSpec...  3.41 us

profile of v11, /device:TPU:0, one launch (start us, length us, event | category | flops | bytes accessed | tf_op | source)
XLA Modules:
  0.0 61.8 jit_solution(11069022205205609435)
XLA Ops:
  0.6 57.7 %outer_step.1 = (f32[1024,8,128]{2,1,0:T(8,128)S(1)}, f32[1024,8,128]{2,1,0:T(8,128)S(1)}) custom-call(f32[1024,8,128]{2,1,0:T(8,128)} %bitcast.25, f32[1024,8,128]{2,1,0:T(8,128)} %bitcast.26, f32[1024,8,128]{2,1,0:T(8,128)} %bitcast.27), custom_call_target="tpu_custom_call" | custom-call | tf_op jit(solution)/shard_map/outer_step/pallas_call | solution.py:502
  58.4 3.4 %store.1 = (f32[1024,8,128]{2,1,0:T(8,128)}, f32[1024,8,128]{2,1,0:T(8,128)}) custom-call(f32[1024,8,128]{2,1,0:T(8,128)S(1)} %get-tuple-element.6.params, f32[1024,8,128]{2,1,0:T(8,128)S(1)} %get-tuple-element.7.momentum), custom_call_target="tpu_custom_call" | custom-call | tf_op jit(solution)/shard_map/store/pallas_call | solution.py:539
